TPU v7x, 32 devices: a whole 2x2x4 slice. The times are simulated.
32 devices in a mesh: frame: 8 (over z, core), video: 4 (over y, x).
Axes of the slice: x: 2, y: 2, z: 4, core: 2. Of those that a mesh axis runs over, the one named last changes fastest.
Arguments:
- video: bfloat16 [24, 8, 197, 768], P('video', 'frame'), may hold values from -6 to 6
- video_live: int32 [24], P('video'), may hold values 0 or 1
- cotangent: bfloat16 [24, 8, 198, 768], P('video', 'frame'), may hold values from -6 to 6
- message_proj: bfloat16 [768, 768], replicated, may hold values from -0.21875 to 0.21875
- message_bias: float32 [768], replicated, may hold values from -3 to 3
- message_gain: float32 [768], replicated, may hold values from 0.5 to 1.5
- message_shift: float32 [768], replicated, may hold values from -1.75 to 1.75
- message_qkv: bfloat16 [768, 2304], replicated, may hold values from -0.21875 to 0.21875
- message_out: bfloat16 [768, 768], replicated, may hold values from -0.4375 to 0.4375
- frame_gain: float32 [768], replicated, may hold values from 0.5 to 1.5
- frame_shift: float32 [768], replicated, may hold values from -1.75 to 1.75
- frame_qkv: bfloat16 [768, 2304], replicated, may hold values from -0.21875 to 0.21875
- frame_out: bfloat16 [768, 768], replicated, may hold values from -0.875 to 0.875
- dense_gain: float32 [768], replicated, may hold values from 0.5 to 1.5
- dense_shift: float32 [768], replicated, may hold values from -1.75 to 1.75
- dense_in: bfloat16 [768, 3072], replicated, may hold values from -0.21875 to 0.21875
- dense_in_bias: float32 [3072], replicated, may hold values from -3 to 3
- dense_out: bfloat16 [3072, 768], replicated, may hold values from -0.21875 to 0.21875
- dense_out_bias: float32 [768], replicated, may hold values from -3 to 3
Outputs:
- output: bfloat16 [24, 8, 198, 768], P('video', 'frame')
- grad_video: bfloat16 [24, 8, 197, 768], P('video', 'frame')
- grad_message_proj: float32 [768, 768], P('video')
- grad_message_bias: float32 [768], P('video')
- grad_message_gain: float32 [768], P('video')
- grad_message_shift: float32 [768], P('video')
- grad_message_qkv: float32 [768, 2304], P('video')
- grad_message_out: float32 [768, 768], P('video')
- grad_frame_gain: float32 [768], P('video')
- grad_frame_shift: float32 [768], P('video')
- grad_frame_qkv: float32 [768, 2304], P('video')
- grad_frame_out: float32 [768, 768], P('video')
- grad_dense_gain: float32 [768], P('video')
- grad_dense_shift: float32 [768], P('video')
- grad_dense_in: float32 [768, 3072], P('video')
- grad_dense_in_bias: float32 [3072], P('video')
- grad_dense_out: float32 [3072, 768], P('video')
- grad_dense_out_bias: float32 [768], P('video')
Inputs may be any that keep to these rules, and one draw needn't show every extreme that they name: `video_live`: 1 marks a video whose output gradient counts, 0 a padded slot.
All inputs are finite; a program needn't handle non-finite values. No bound on the sum of `video_live` on one device may be relied on, other than what follows from the above.
Results may differ from a plain program's by a relative error of at most 0.025.
Values may be sent and summed in bfloat16 or wider, within the bound.
A program may use at most 192 MiB of HBM per device.

v0:
```python
import functools
import jax
import jax.numpy as jnp
from jax import lax
from jax.experimental import pallas as pl
from jax.experimental.pallas import tpu as pltpu
bf=jnp.bfloat16; f32=jnp.float32
EPS=1e-5
def dot(a,b,ca=1,cb=0): return lax.dot_general(a,b,(((ca,),(cb,)),((),())),preferred_element_type=f32)
FR=6; T=208; RR=FR*T; RP=1280; D=768
def k2(MB, mid, cot, live, din0,din1,din2,din3, do0,do1,do2,do3, bin_, bout, gain, shift,
       out_ref, gmid_ref, gdi_ref, gdo_ref, gbin_ref, small_ref,
       sec, G, act, dinn, oacc, gsec):
    j=pl.program_id(0)
    @pl.when(j==0)
    def _():
        ob=jnp.zeros((1,D),f32)
        sec[pl.ds(RR,RP-RR),:]=jnp.zeros((RP-RR,D),bf)
        G[pl.ds(RR,RP-RR),:]=jnp.zeros((RP-RR,D),bf)
        act[pl.ds(RR,RP-RR),:]=jnp.zeros((RP-RR,512),bf)
        dinn[pl.ds(RR,RP-RR),:]=jnp.zeros((RP-RR,512),bf)
        for f in range(FR):
            x=mid[f*T:(f+1)*T,:]
            mu=jnp.mean(x,-1,keepdims=True); c=x-mu
            inv=lax.rsqrt(jnp.mean(c*c,-1,keepdims=True)+EPS)
            sec[f*T:(f+1)*T,:]=(c*inv*gain[...]+shift[...]).astype(bf)
            g=cot[f,0].astype(f32)*live[f].astype(f32)
            g=jnp.concatenate([g,jnp.zeros((T-198,D),f32)],0)
            ob=ob+jnp.sum(g,0,keepdims=True)
            G[f*T:(f+1)*T,:]=g.astype(bf)
            oacc[f*T:(f+1)*T,:]=x+bout[...]
            gsec[f*T:(f+1)*T,:]=jnp.zeros((T,D),f32)
        small_ref[0:1,:]=ob
    din=jnp.concatenate([din0[...],din1[...],din2[...],din3[...]],1)
    do=jnp.concatenate([do0[...],do1[...],do2[...],do3[...]],0)
    b=jnp.concatenate([bin_[0:1,:],bin_[1:2,:],bin_[2:3,:],bin_[3:4,:]],1) if False else bin_[0]
    bsum=jnp.zeros((1,512),f32)
    for r in range(RR//MB):
        s=slice(r*MB,(r+1)*MB)
        inner=dot(sec[s,:],din)+b
        ga=dot(G[s,:],do,1,1)
        sg=0.5*jnp.tanh(0.851*inner)+0.5
        ac=inner*sg
        act[s,:]=ac.astype(bf)
        di=ga*(sg+1.702*ac*(1.0-sg))
        bsum=bsum+jnp.sum(di,0,keepdims=True)
        dinn[s,:]=di.astype(bf)
    gbin_ref[0]=bsum
    for r in range(RR//MB):
        s=slice(r*MB,(r+1)*MB)
        oacc[s,:]+=dot(act[s,:],do)
        gsec[s,:]+=dot(dinn[s,:],din,1,1)
    gdo_ref[0]=dot(G[...],act[...],0,0).astype(bf)
    gdi_ref[0]=dot(sec[...],dinn[...],0,0).astype(bf)
    @pl.when(j==pl.num_programs(0)-1)
    def _():
        gg=jnp.zeros((1,D),f32); gs=jnp.zeros((1,D),f32)
        for f in range(FR):
            s=slice(f*T,(f+1)*T)
            out_ref[f,0]=oacc[s,:][:198].astype(bf)
            x=mid[s,:]
            mu=jnp.mean(x,-1,keepdims=True); c=x-mu
            inv=lax.rsqrt(jnp.mean(c*c,-1,keepdims=True)+EPS)
            sc=c*inv
            go=gsec[s,:]
            gg=gg+jnp.sum(go*sc,0,keepdims=True); gs=gs+jnp.sum(go,0,keepdims=True)
            gsc=go*gain[...]
            gi=inv*(gsc-jnp.mean(gsc,-1,keepdims=True)-sc*jnp.mean(gsc*sc,-1,keepdims=True))
            gmid_ref[s,:]=G[s,:].astype(f32)+gi
        small_ref[1:2,:]=gg; small_ref[2:3,:]=gs
def call_k2(mid,cot,live,din,do,bin_,bout,gain,shift,MB=624):
    full=lambda *s: pl.BlockSpec(s,lambda j:(0,)*len(s))
    nq=din.shape[1]//512
    vm=pl.BlockSpec(memory_space=pltpu.VMEM)
    specs=[full(RR,D),full(FR,1,198,D),pl.BlockSpec(memory_space=pltpu.SMEM)]
    for q in range(4): specs.append(pl.BlockSpec((D,128),lambda j,q=q:(0,q*6+j)))
    for q in range(4): specs.append(pl.BlockSpec((128,D),lambda j,q=q:(q*6+j,0)))
    specs+= [pl.BlockSpec((1,1,512),lambda j:(j,0,0)),full(1,D),full(1,D),full(1,D)]
    b3=bin_.reshape(4,6,128).transpose(1,0,2).reshape(6,1,512)
    return pl.pallas_call(functools.partial(k2,MB),grid=(6,),in_specs=specs,
      out_specs=[full(FR,1,198,D),full(RR,D),pl.BlockSpec((1,D,512),lambda j:(j,0,0)),pl.BlockSpec((1,D,512),lambda j:(j,0,0)),pl.BlockSpec((1,1,512),lambda j:(j,0,0)),full(8,D)],
      out_shape=[jax.ShapeDtypeStruct((FR,1,198,D),bf),jax.ShapeDtypeStruct((RR,D),f32),jax.ShapeDtypeStruct((6,D,512),bf),jax.ShapeDtypeStruct((6,D,512),bf),jax.ShapeDtypeStruct((6,1,512),f32),jax.ShapeDtypeStruct((8,D),f32)],
      scratch_shapes=[pltpu.VMEM((RP,D),bf),pltpu.VMEM((RP,D),bf),pltpu.VMEM((RP,512),bf),pltpu.VMEM((RP,512),bf),pltpu.VMEM((RR,D),f32),pltpu.VMEM((RR,D),f32)],
      compiler_params=pltpu.CompilerParams(vmem_limit_bytes=61<<20,dimension_semantics=("arbitrary",)),
    )(mid,cot,live,din,din,din,din,do,do,do,do,b3,bout.reshape(1,D),gain.reshape(1,D),shift.reshape(1,D))
from jax.sharding import PartitionSpec as P
HEADS=12
HEAD_DIM=64
NEG=-1e30
VMEM_LIMIT=63<<20

def half_masks(rows):
    lane=lax.broadcasted_iota(jnp.int32,(rows,128),1)
    return lane<64
def attend_frames(h,wq,wk,wv,wo,qkv_ref,pt_ref,first_ref,mixed_ref,mid_ref):
    w=jnp.concatenate([wq[...],wk[...],wv[...]],1)
    qkv_ref[0,0:RR,:]=dot(first_ref[0:RR,:],w).astype(bf)
    qkv_ref[0,RR:RP,:]=jnp.zeros((RP-RR,384),bf)
    lo=half_masks(T)
    keep=lax.broadcasted_iota(jnp.int32,(16,T),0)<6
    zero=jnp.zeros((T,128),bf)
    def one(f,carry):
        s=pl.ds(pl.multiple_of(f*T,16),T)
        q=qkv_ref[0,s,0:128]*jnp.asarray(0.125,bf); k=qkv_ref[0,s,128:256]; v=qkv_ref[0,s,256:384]
        ps=[]; vs=[]
        for e in range(2):
            m=lo if e==0 else jnp.logical_not(lo)
            st=dot(k,jnp.where(m,q,zero),1,1)
            top=st[:192]; bot=jnp.where(keep,st[192:],NEG)
            mx=jnp.maximum(jnp.max(top,0,keepdims=True),jnp.max(bot,0,keepdims=True))
            top=jnp.exp(top-mx); bot=jnp.exp(bot-mx)
            tot=jnp.sum(top,0,keepdims=True)+jnp.sum(bot,0,keepdims=True)
            p=(jnp.concatenate([top,bot],0)*(1.0/tot)).astype(bf)
            pt_ref[0,f*2+e]=p
            ps.append(p); vs.append(jnp.where(m,v,zero))
        o=dot(jnp.concatenate(ps,0),jnp.concatenate(vs,0),0,0)
        mixed_ref[s,pl.ds(pl.multiple_of(h*128,128),128)]=o.astype(bf)
        return carry
    lax.fori_loop(0,FR,one,0,unroll=True)
    @pl.when(h==5)
    def _():
        mid_ref[...]+=dot(mixed_ref[0:RR,:],wo[...])
def k1(vid, mnext, wq, wk, wv, wo, gain, shift,
       qkv_ref, pt_ref, first_ref, mixed_ref, mid_ref, tok_ref):
    h=pl.program_id(0)
    @pl.when(h==0)
    def _():
        first_ref[pl.ds(RR,RP-RR),:]=jnp.zeros((RP-RR,D),bf)
        mixed_ref[pl.ds(RR,RP-RR),:]=jnp.zeros((RP-RR,D),bf)
        for f in range(FR):
            mid_ref[f*T+192:(f+1)*T,:]=jnp.zeros((T-192,D),f32)
            mid_ref[f*T:f*T+197,:]=vid[f,0].astype(f32)
            mid_ref[f*T+197:f*T+198,:]=mnext[f:f+1,:]
            x=mid_ref[f*T:(f+1)*T,:]
            tok_ref[f*T:(f+1)*T,:]=x.astype(bf)
            mu=jnp.mean(x,-1,keepdims=True); c=x-mu
            inv=lax.rsqrt(jnp.mean(c*c,-1,keepdims=True)+EPS)
            first_ref[f*T:(f+1)*T,:]=(c*inv*gain[...]+shift[...]).astype(bf)
    attend_frames(h,wq,wk,wv,wo,qkv_ref,pt_ref,first_ref,mixed_ref,mid_ref)
def call_k1(video,mnext,qkv,wo,gain,shift):
    full=lambda *s: pl.BlockSpec(s,lambda j:(0,)*len(s))
    blk=lambda *s: pl.BlockSpec((1,)+s,lambda j:(j,)+(0,)*len(s))
    specs=[full(FR,1,197,D),full(FR,D)]+[pl.BlockSpec((D,128),lambda j,o=o:(0,o*6+j)) for o in range(3)]+[full(D,D),full(1,D),full(1,D)]
    return pl.pallas_call(k1,grid=(6,),in_specs=specs,
      out_specs=[blk(RP,384),blk(12,T,T),full(RP,D),full(RP,D),full(RR,D),full(RR,D)],
      out_shape=[jax.ShapeDtypeStruct((6,RP,384),bf),jax.ShapeDtypeStruct((6,12,T,T),bf),jax.ShapeDtypeStruct((RP,D),bf),jax.ShapeDtypeStruct((RP,D),bf),jax.ShapeDtypeStruct((RR,D),f32),jax.ShapeDtypeStruct((RR,D),bf)],
      compiler_params=pltpu.CompilerParams(vmem_limit_bytes=61<<20,dimension_semantics=("arbitrary",)),
    )(video,mnext,qkv,qkv,qkv,wo,gain.reshape(1,D),shift.reshape(1,D))
def k3(vid, mnext, gmid, qkv, pt, first, mixed, wq, wk, wv, wo, gain, shift,
       gtok_ref, gf_ref, small_ref, glow, dO, dpk, wqkv):
    h=pl.program_id(0)
    @pl.when(h==0)
    def _():
        glow[pl.ds(RR,RP-RR),:]=jnp.zeros((RP-RR,D),bf)
        dpk[:,pl.ds(RR,RP-RR),:]=jnp.zeros((6,RP-RR,384),bf)
        glow[0:RR,:]=gmid[...].astype(bf)
        d=dot(glow[0:RR,:],wo[...],1,1).astype(bf)
        for i in range(6): dO[i]=d[:,i*128:(i+1)*128]
    lo=half_masks(T)
    zero=jnp.zeros((T,128),bf)
    for f in range(FR):
        s=slice(f*T,(f+1)*T)
        q=qkv[0,s,0:128]; k=qkv[0,s,128:256]; v=qkv[0,s,256:384]
        do=dO[h,s,:]
        dss=[]; ks=[]; dk=0.; dv=0.
        for e in range(2):
            m=lo if e==0 else jnp.logical_not(lo)
            doe=jnp.where(m,do,zero)
            pb=pt[0,f*2+e]
            p=pb.astype(f32)
            dp=dot(v,doe,1,1)
            delta=jnp.sum(dp*p,0,keepdims=True)
            ds=(p*(dp-delta)).astype(bf)
            dk=dk+dot(ds,jnp.where(m,q,zero))
            dv=dv+dot(pb,doe)
            dss.append(ds); ks.append(jnp.where(m,k,zero))
        dq=dot(jnp.concatenate(dss,0),jnp.concatenate(ks,0),0,0)*0.125
        dpk[h,s,0:128]=dq.astype(bf)
        dpk[h,s,128:256]=(dk*0.125).astype(bf)
        dpk[h,s,256:384]=dv.astype(bf)
    for i in range(6):
        @pl.when(h==i)
        def _():
            wqkv[:,i*128:(i+1)*128]=wq[...]; wqkv[:,D+i*128:D+(i+1)*128]=wk[...]; wqkv[:,2*D+i*128:2*D+(i+1)*128]=wv[...]
            gf_ref[0,:,384:512]=dot(mixed[...],glow[:,i*128:(i+1)*128],0,0).astype(bf)
    gf_ref[0,:,0:384]=dot(first[...],dpk[h],0,0).astype(bf)
    @pl.when(h==5)
    def _():
        dx=jnp.concatenate([dpk[i,0:RR,g*128:(g+1)*128] for g in range(3) for i in range(6)],1)
        gtok_ref[...]=dot(dx,wqkv[...],1,1)
        gg=jnp.zeros((1,D),f32); gs=jnp.zeros((1,D),f32)
        for f in range(FR):
            s=slice(f*T,(f+1)*T)
            x=jnp.concatenate([vid[f,0].astype(f32),mnext[f:f+1,:],jnp.zeros((T-198,D),f32)],0)
            mu=jnp.mean(x,-1,keepdims=True); c=x-mu
            inv=lax.rsqrt(jnp.mean(c*c,-1,keepdims=True)+EPS)
            sc=c*inv
            go=gtok_ref[s,:]
            gg=gg+jnp.sum(go*sc,0,keepdims=True); gs=gs+jnp.sum(go,0,keepdims=True)
            gsc=go*gain[...]
            gi=inv*(gsc-jnp.mean(gsc,-1,keepdims=True)-sc*jnp.mean(gsc*sc,-1,keepdims=True))
            gtok_ref[s,:]=gmid[s,:]+gi
        small_ref[0:1,:]=gg; small_ref[1:2,:]=gs
def call_k3(video,mnext,gmid,qkvs,pt,first,mixed,qkv,wo,gain):
    full=lambda *s: pl.BlockSpec(s,lambda j:(0,)*len(s))
    blk=lambda *s: pl.BlockSpec((1,)+s,lambda j:(j,)+(0,)*len(s))
    specs=[full(FR,1,197,D),full(FR,D),full(RR,D),blk(RP,384),blk(12,T,T),full(RP,D),full(RP,D)]+[pl.BlockSpec((D,128),lambda j,o=o:(0,o*6+j)) for o in range(3)]+[full(D,D),full(1,D),full(1,D)]
    return pl.pallas_call(k3,grid=(6,),in_specs=specs,
      out_specs=[full(RR,D),blk(D,512),full(8,D)],
      out_shape=[jax.ShapeDtypeStruct((RR,D),f32),jax.ShapeDtypeStruct((6,D,512),bf),jax.ShapeDtypeStruct((8,D),f32)],
      scratch_shapes=[pltpu.VMEM((RP,D),bf),pltpu.VMEM((6,RR,128),bf),pltpu.VMEM((6,RP,384),bf),pltpu.VMEM((D,3*D),bf)],
      compiler_params=pltpu.CompilerParams(vmem_limit_bytes=61<<20,dimension_semantics=("arbitrary",)),
    )(video,mnext,gmid,qkvs,pt,first,mixed,qkv,qkv,qkv,wo,gain.reshape(1,D),gain.reshape(1,D))


UNITS = 18
DENSE_UNITS = 12
STEPS = 12
LAG = (0, 1, 3, 5, 7, 9, 11, 13, 15)
ROWS = 192


def add_norm_stats(values):
    mean = jnp.mean(values, -1, keepdims=True)
    center = values - mean
    inverse = lax.rsqrt(jnp.mean(center * center, -1, keepdims=True) + EPS)
    return center * inverse, inverse


def norm_back(grad, scaled, inverse, gain):
    grad_scaled = grad * gain
    return inverse * (
        grad_scaled
        - jnp.mean(grad_scaled, -1, keepdims=True)
        - scaled * jnp.mean(grad_scaled * scaled, -1, keepdims=True)
    )


def pack_rows(values):
    return jnp.concatenate([values[:, : D // 2], values[:, D // 2 :]], 0).astype(bf)


def unpack_rows(blocks):
    wide = blocks.astype(f32)
    rows = jnp.concatenate([wide[:, :8], wide[:, 8:]], 2)
    return rows.reshape(rows.shape[0] * 8, D)


def gather_moves(B, ssem, rsem, f_at, v_at):
    me = v_at * 8 + f_at

    def move(k, src, target):
        return pltpu.make_async_remote_copy(
            src_ref=src,
            dst_ref=src,
            send_sem=ssem.at[k],
            recv_sem=rsem.at[k],
            device_id=target,
            device_id_type=pl.DeviceIdType.MESH,
        )

    def near():
        return [move(i - 1, B.at[me], (lax.rem(f_at + i, 8), v_at)) for i in range(1, 8)]

    def far():
        x, y = lax.rem(v_at, 2), lax.div(v_at, 2)
        block = B.at[pl.ds(v_at * 8, 8)]
        xo, yo = v_at + 1 - 2 * x, v_at + 2 - 4 * y
        return [move(7 + i, block, (f_at, to)) for i, to in enumerate((xo, yo, 3 - v_at))]

    return near, far


def greet(f_at, v_at):
    x, y = lax.rem(v_at, 2), lax.div(v_at, 2)
    barrier = pltpu.get_barrier_semaphore()
    others = [(lax.rem(f_at + i, 8), v_at) for i in range(1, 8)]
    others += [(f_at, to) for to in (v_at + 1 - 2 * x, v_at + 2 - 4 * y, 3 - v_at)]
    for other in others:
        pl.semaphore_signal(barrier, inc=1, device_id=other, device_id_type=pl.DeviceIdType.MESH)
    return lambda: pl.semaphore_wait(barrier, 10)


def message_rows(cls, proj, bias):
    return (dot(cls, proj) + bias).astype(bf).astype(f32)


def attend_rows(packed, mask, rows):
    lo = lax.broadcasted_iota(jnp.int32, (rows, 128), 1) < 64
    zero = jnp.zeros((rows, 128), bf)
    out, kept = [], []
    for h in range(6):
        q = packed[:, h * 128 : (h + 1) * 128] * jnp.asarray(0.125, bf)
        k = packed[:, D + h * 128 : D + (h + 1) * 128]
        v = packed[:, 2 * D + h * 128 : 2 * D + (h + 1) * 128]
        ps, vs = [], []
        for e in range(2):
            m = lo if e == 0 else jnp.logical_not(lo)
            st = jnp.where(mask, dot(k, jnp.where(m, q, zero), 1, 1), NEG)
            raised = jnp.exp(st - jnp.max(st, 0, keepdims=True))
            p = (raised * (1.0 / jnp.sum(raised, 0, keepdims=True))).astype(bf)
            ps.append(p)
            vs.append(jnp.where(m, v, zero))
        kept += ps
        out.append(dot(jnp.concatenate(ps, 0), jnp.concatenate(vs, 0), 0, 0).astype(bf))
    return jnp.concatenate(out, 1), kept


def first_kernel(
    vid, wq, wk, wv, wo, gain, shift, mproj_h, mqkv_h, mout_h, mbias, mgain, mshift,
    qkv_ref, pt_ref, first_ref, mixed_ref, mid_ref, tok_ref, mnext_ref, cls_ref,
    mproj, mqkv, mout, B, mrows, wsem, ssem, rsem,
):
    h = pl.program_id(0)
    f_at, v_at = lax.axis_index("frame"), lax.axis_index("video")
    near, far = gather_moves(B, ssem, rsem, f_at, v_at)

    def put_rows(rows, values):
        scaled, _ = add_norm_stats(values)
        first_ref[rows, :] = (scaled * gain[...] + shift[...]).astype(bf)
        tok_ref[rows, :] = values.astype(bf)

    @pl.when(h == 0)
    def _():
        loads = [
            pltpu.make_async_copy(src, dst, wsem.at[i])
            for i, (src, dst) in enumerate(((mproj_h, mproj), (mqkv_h, mqkv), (mout_h, mout)))
        ]
        arrived = greet(f_at, v_at)
        for load in loads:
            load.start()
        own = jnp.concatenate([vid[f, 0, 0:1].astype(f32) for f in range(FR)] + [jnp.zeros((8 - FR, D), f32)], 0)
        B[v_at * 8 + f_at] = pack_rows(own)
        arrived()
        sends = near()
        for send in sends:
            send.start()
        first_ref[pl.ds(RR, RP - RR), :] = jnp.zeros((RP - RR, D), bf)
        mixed_ref[pl.ds(RR, RP - RR), :] = jnp.zeros((RP - RR, D), bf)
        def begin(f, rows, carry):
            mid_ref[rows, :] = jnp.concatenate([vid[f, 0].astype(f32), jnp.zeros((T - 197, D), f32)], 0)
            rows = pl.ds(pl.multiple_of(f * T, 16), 192)
            put_rows(rows, mid_ref[rows, :])
            return carry

        frames_loop(begin, 0)
        for load in loads:
            load.wait()
        for send in sends:
            send.wait()
        for send in far():
            send.start()
        cls = unpack_rows(B[pl.ds(v_at * 8, 8)]).astype(bf)
        message = message_rows(cls, mproj[...], mbias[...])
        scaled, _ = add_norm_stats(message)
        packed = dot((scaled * mgain[...] + mshift[...]).astype(bf), mqkv[...]).astype(bf)
        same = lax.rem(lax.broadcasted_iota(jnp.int32, (64, 64), 0), 8) == lax.rem(
            lax.broadcasted_iota(jnp.int32, (64, 64), 1), 8
        )
        mixed, _ = attend_rows(packed, same, 64)
        mrows[...] = message + dot(mixed, mout[...])
        mnext_ref[...] = mrows[pl.ds(pl.multiple_of(f_at * 8, 8), 8), :]
        last_row = lax.broadcasted_iota(jnp.int32, (16, D), 0) == 5

        def finish(f, rows, carry):
            rows = pl.ds(pl.multiple_of(f * T + 192, 16), 16)
            values = jnp.where(last_row, mnext_ref[pl.ds(f, 1), :], mid_ref[rows, :])
            mid_ref[rows, :] = values
            put_rows(rows, values)
            return carry

        frames_loop(finish, 0)

    attend_frames(h, wq, wk, wv, wo, qkv_ref, pt_ref, first_ref, mixed_ref, mid_ref)

    @pl.when(h == 5)
    def _():
        for send in far():
            send.wait()
        cls_ref[...] = B[...]


def call_first(video, qkv, wo, gain, shift, mproj, mbias, mgain, mshift, mqkv, mout):
    one = pl.Buffered(1)
    full = lambda *s: pl.BlockSpec(s, lambda j: (0,) * len(s), pipeline_mode=one)
    keep = lambda *s: pl.BlockSpec(s, lambda j: (0,) * len(s))
    blk = lambda *s: pl.BlockSpec((1,) + s, lambda j: (j,) + (0,) * len(s))
    hbm = pl.BlockSpec(memory_space=pl.ANY)
    specs = [full(FR, 1, 197, D)] + [pl.BlockSpec((D, 128), lambda j, o=o: (0, o * 6 + j)) for o in range(3)]
    specs += [full(D, D), full(D), full(D), hbm, hbm, hbm, full(D), full(D), full(D)]
    shape = jax.ShapeDtypeStruct
    dma = pltpu.SemaphoreType.DMA
    return pl.pallas_call(
        first_kernel,
        grid=(6,),
        in_specs=specs,
        out_specs=[
            blk(RP, 384), blk(12, T, T), keep(RP, D), keep(RP, D), keep(RR, D), keep(RR, D), keep(8, D),
            keep(32, 16, D // 2),
        ],
        out_shape=[
            shape((6, RP, 384), bf),
            shape((6, 12, T, T), bf),
            shape((RP, D), bf),
            shape((RP, D), bf),
            shape((RR, D), f32),
            shape((RR, D), bf),
            shape((8, D), f32),
            shape((32, 16, D // 2), bf),
        ],
        scratch_shapes=[
            pltpu.VMEM((D, D), bf),
            pltpu.VMEM((D, 3 * D), bf),
            pltpu.VMEM((D, D), bf),
            pltpu.VMEM((32, 16, D // 2), bf),
            pltpu.VMEM((64, D), f32),
            dma((3,)),
            dma((10,)),
            dma((10,)),
        ],
        compiler_params=pltpu.CompilerParams(
            vmem_limit_bytes=VMEM_LIMIT, dimension_semantics=("arbitrary",), collective_id=2, has_side_effects=True
        ),
    )(video, qkv, qkv, qkv, wo, gain, shift, mproj, mqkv, mout, mbias, mgain, mshift)


MROWS = 256


def rows_back(MP, PR, GM, GP, heads):
    lo = lax.broadcasted_iota(jnp.int32, (MROWS, 128), 1) < 64
    zero = jnp.zeros((MROWS, 128), bf)
    for h in heads:
        q, k, v = (MP[:, o * D + h * 128 : o * D + (h + 1) * 128] for o in range(3))
        do = GM[:, h * 128 : (h + 1) * 128]
        dss, ks, dk, dv = [], [], 0.0, 0.0
        for e in range(2):
            m = lo if e == 0 else jnp.logical_not(lo)
            doe = jnp.where(m, do, zero)
            pb = PR[2 * h + e]
            p = pb.astype(f32)
            dp = dot(v, doe, 1, 1)
            ds = (p * (dp - jnp.sum(dp * p, 0, keepdims=True))).astype(bf)
            dk = dk + dot(ds, jnp.where(m, q, zero))
            dv = dv + dot(pb, doe)
            dss.append(ds)
            ks.append(jnp.where(m, k, zero))
        dq = dot(jnp.concatenate(dss, 0), jnp.concatenate(ks, 0), 0, 0) * 0.125
        for o, part in enumerate((dq, dk * 0.125, dv)):
            GP[:, o * D + h * 128 : o * D + (h + 1) * 128] = part.astype(bf)


def frames_loop(body, carry):
    def step(f, carry):
        return body(f, pl.ds(pl.multiple_of(f * T, 16), T), carry)

    return lax.fori_loop(0, FR, step, carry)


def exchange(tick, where, U, RA, RB, RC, RD, RE, F, ssem, rsem, fsem, F_out):
    c, x, y, z0, z1, core, xn, yn, zn, zf = where

    def at(lag_dense, lag_frame, body):
        dense = tick - lag_dense
        late = tick - lag_frame - 13
        step = lax.div(jnp.maximum(late, 0), 2)
        is_dense = jnp.logical_and(dense >= 0, dense < 12)
        is_frame = jnp.logical_and(jnp.logical_and(late >= 0, lax.rem(jnp.maximum(late, 0), 2) == 0), step < 6)

        @pl.when(is_dense)
        def _():
            body(jnp.clip(dense, 0, 11))

        @pl.when(is_frame)
        def _():
            body(12 + jnp.minimum(step, 5))

    def move(g, k, src, dst, target):
        return pltpu.make_async_remote_copy(
            src_ref=src,
            dst_ref=dst,
            send_sem=ssem.at[g, k],
            recv_sem=rsem.at[g, k],
            device_id=target,
            device_id_type=pl.DeviceIdType.MESH,
        )

    def a(g):
        return move(g, 0, U.at[lax.rem(g, 2), :, :, pl.ds(2 * (1 - c), 2)], RA.at[lax.rem(g, 6)], core)

    def b0(g):
        return move(g, 1, RA.at[lax.rem(g, 6), :, 1 - x, 0], RB.at[lax.rem(g, 8), 0], xn)

    def b1(g):
        return move(g, 2, RA.at[lax.rem(g, 6), 1 - y, :, 1], RB.at[lax.rem(g, 8), 1], yn)

    def c0(g):
        return move(g, 3, RB.at[lax.rem(g, 8), 0, 1 - y], RC.at[lax.rem(g, 8), 0], yn)

    def c1(g):
        return move(g, 4, RB.at[lax.rem(g, 8), 1, 1 - x], RC.at[lax.rem(g, 8), 1], xn)

    def d1(g):
        return move(g, 5, RC.at[lax.rem(g, 8), 1 - z0], RD.at[g], zn)

    def d2(g):
        return move(g, 6, RD.at[g, pl.ds((1 - z1) * 96, 96)], RE.at[g], zf)

    def e2(g):
        piece = F.at[g, 2 * c + z0, pl.ds(z1 * 96, 96)]
        return move(g, 7, piece, piece, zf)

    def e1(g):
        piece = F.at[g, 2 * c + z0]
        return move(g, 8, piece, piece, zn)

    def last(g):
        piece = F.at[g, pl.ds(2 * c, 2)]
        return move(g, 9, piece, piece, core)

    def on_done(g):
        last(g).wait()
        pltpu.make_async_copy(F.at[g], F_out.at[g], fsem.at[g]).start()

    def on_last(g):
        e1(g).wait()
        last(g).start()

    def on_e1(g):
        e2(g).wait()
        e1(g).start()

    def on_e2(g):
        d2(g).wait()
        own = pl.ds(z1 * 96, 96)
        F[g, 2 * c + z0, own] = RE[g] + RD[g, own]
        e2(g).start()

    def on_d2(g):
        d1(g).wait()
        RD[g] = RD[g] + RC[lax.rem(g, 8), z0]
        d2(g).start()

    def on_d1(g):
        c0(g).wait()
        c1(g).wait()
        RC[lax.rem(g, 8), 0] = RC[lax.rem(g, 8), 0] + RB[lax.rem(g, 8), 0, y]
        RC[lax.rem(g, 8), 1] = RC[lax.rem(g, 8), 1] + RB[lax.rem(g, 8), 1, x]
        d1(g).start()

    def on_c(g):
        b0(g).wait()
        b1(g).wait()
        RB[lax.rem(g, 8), 0] = RB[lax.rem(g, 8), 0] + RA[lax.rem(g, 6), :, x, 0]
        RB[lax.rem(g, 8), 1] = RB[lax.rem(g, 8), 1] + RA[lax.rem(g, 6), y, :, 1]
        c0(g).start()
        c1(g).start()

    def on_b(g):
        a(g).wait()
        RA[lax.rem(g, 6)] = RA[lax.rem(g, 6)] + U[lax.rem(g, 2), :, :, pl.ds(2 * c, 2)]
        b0(g).start()
        b1(g).start()

    def on_a(g):
        a(g).start()

    bodies = (on_a, on_b, on_c, on_d1, on_d2, on_e2, on_e1, on_last, on_done)
    for lag, body in zip(LAG, bodies):
        at(lag, lag, body)


def main_kernel(
    mid, cot, live, din0, din1, din2, din3, do0, do1, do2, do3, bin_, bout, gain2, shift2,
    qkv, pt, wq, wk, wv, first_hbm, mixed_hbm, wo_hbm, tok_hbm, mnext, gain1,
    mproj_hbm, mqkv_hbm, mout_hbm, cls_hbm, mbias, mgain, mshift,
    out_hbm, gt_hbm, F_out, gp_out, lr_out, edge_out,
    sec, G, act, dinn, oacc, gsec, CB, first, mixed, wo, dpk,
    U, RA, RB, RC, RD, RE, F, BI, SB, NB, AD, AN, AS, mv, CLS, MP, PR, MS, GP, GM, LR, EDGE, HELD, ssem, rsem, fsem, lsem, adsem, adrem, ansem, anrem, assem, asrem,
):
    t = pl.program_id(0)
    f_at, v_at = lax.axis_index("frame"), lax.axis_index("video")
    c, z = lax.rem(f_at, 2), lax.div(f_at, 2)
    x, y = lax.rem(v_at, 2), lax.div(v_at, 2)
    z0, z1 = lax.rem(z, 2), lax.div(z, 2)
    core = (f_at + 1 - 2 * c, v_at)
    xn = (f_at, v_at + 1 - 2 * x)
    yn = (f_at, v_at + 2 - 4 * y)
    zn = (f_at + 2 - 4 * z0, v_at)
    zf = (f_at + 4 - 8 * z1, v_at)
    where = (c, x, y, z0, z1, core, xn, yn, zn, zf)

    small_near, small_far = gather_moves(AD, adsem, adrem, f_at, v_at)
    next_near, next_far = gather_moves(AN, ansem, anrem, f_at, v_at)
    sums_near, sums_far = gather_moves(AS, assem, asrem, f_at, v_at)

    def tick(n):
        exchange(n, where, U, RA, RB, RC, RD, RE, F, ssem, rsem, fsem, F_out)

    def fetch(k):
        src, dst = (
            (first_hbm, first),
            (mixed_hbm, mixed),
            (wo_hbm, wo),
            (tok_hbm, act.at[pl.ds(0, RR)]),
            (CB, out_hbm),
            (sec.at[pl.ds(0, RR)], gt_hbm),
            (cot, CB),
            (GP, gp_out),
            (LR, lr_out),
            (EDGE, edge_out),
            (mproj_hbm, G.at[pl.ds(0, D)]),
            (mqkv_hbm.at[:, pl.ds(0, D)], first.at[pl.ds(0, D)]),
            (mqkv_hbm.at[:, pl.ds(D, D)], mixed.at[pl.ds(0, D)]),
            (mqkv_hbm.at[:, pl.ds(2 * D, D)], mv),
            (mout_hbm, wo),
            (cls_hbm, CLS),
        )[k]
        return pltpu.make_async_copy(src, dst, lsem.at[k])

    tail = pl.ds(RR, RP - RR)

    @pl.when(t == 0)
    def _():
        fetch(6).start()
        arrived = greet(f_at, v_at)
        for k in range(3):
            fetch(k).start()
        sec[tail, :] = jnp.zeros((RP - RR, D), bf)
        G[tail, :] = jnp.zeros((RP - RR, D), bf)
        act[tail, :] = jnp.zeros((RP - RR, D), bf)
        dinn[tail, :] = jnp.zeros((RP - RR, 512), bf)
        dpk[tail, :] = jnp.zeros((RP - RR, 384), bf)
        SB[...] = jnp.zeros((8, D), f32)
        BI[...] = bin_[...].reshape(1, 4 * D)
        def begin(f, rows, carry):
            values = mid[rows, :]
            scaled, _ = add_norm_stats(values)
            sec[rows, :] = (scaled * gain2[...] + shift2[...]).astype(bf)
            oacc[rows, :] = values + bout[...]
            gsec[rows, :] = jnp.zeros((T, D), f32)
            return carry

        frames_loop(begin, 0)
        fetch(6).wait()

        def weigh(f, rows, total):
            grad = CB[f, 0].astype(f32) * live[f].astype(f32)
            G[rows, :] = jnp.concatenate([grad, jnp.zeros((T - 198, D), f32)], 0).astype(bf)
            return total + jnp.sum(grad, 0, keepdims=True)

        SB[4:5, :] = frames_loop(weigh, jnp.zeros((1, D), f32))
        arrived()

    din = lambda: jnp.concatenate([din0[...], din1[...], din2[...], din3[...]], 1)
    dout = lambda: jnp.concatenate([do0[...], do1[...], do2[...], do3[...]], 0)

    def put(slot, index, block):
        q, b = index
        U[slot, q // 2, q % 2, b] = block.astype(bf)

    @pl.when(t < 6)
    def _():
        w_in, w_out = din(), dout()
        bias = jnp.concatenate([BI[:, pl.ds(pl.multiple_of(q * D + t * 128, 128), 128)] for q in range(4)], 1)
        sums = jnp.zeros((1, 512), f32)
        MB = 416
        for r in range(RR // MB):
            s = slice(r * MB, (r + 1) * MB)
            inner = dot(sec[s, :], w_in) + bias
            ga = dot(G[s, :], w_out, 1, 1)
            sg = 0.5 * jnp.tanh(0.851 * inner) + 0.5
            ac = inner * sg
            act[s, 0:512] = ac.astype(bf)
            di = ga * (sg + 1.702 * ac * (1.0 - sg))
            sums = sums + jnp.sum(di, 0, keepdims=True)
            dinn[s, :] = di.astype(bf)
        for b in range(4):
            SB[b : b + 1, pl.ds(pl.multiple_of(t * 128, 128), 128)] = sums[:, b * 128 : (b + 1) * 128]
        part = dot(G[...], act[:, 0:512], 0, 0)
        for q in range(4):
            for b in range(4):
                put(0, (q, b), part[b * ROWS : (b + 1) * ROWS, q * 128 : (q + 1) * 128])

    lo = lax.broadcasted_iota(jnp.int32, (T, 128), 1) < 64
    zero = jnp.zeros((T, 128), bf)
    head = jnp.maximum(t - 6, 0)
    lanes = pl.ds(pl.multiple_of(head * 128, 128), 128)

    def attend_back(first_frame, count):
        def one(f, carry):
            s = pl.ds(pl.multiple_of(f * T, 16), T)
            q, k, v = qkv[0, s, 0:128], qkv[0, s, 128:256], qkv[0, s, 256:384]
            do = G[s, lanes]
            dss, ks, dk, dv = [], [], 0.0, 0.0
            for e in range(2):
                m = lo if e == 0 else jnp.logical_not(lo)
                doe = jnp.where(m, do, zero)
                pb = pt[0, f * 2 + e]
                p = pb.astype(f32)
                dp = dot(v, doe, 1, 1)
                ds = (p * (dp - jnp.sum(dp * p, 0, keepdims=True))).astype(bf)
                dk = dk + dot(ds, jnp.where(m, q, zero))
                dv = dv + dot(pb, doe)
                dss.append(ds)
                ks.append(jnp.where(m, k, zero))
            dq = dot(jnp.concatenate(dss, 0), jnp.concatenate(ks, 0), 0, 0) * 0.125
            dpk[s, 0:128] = dq.astype(bf)
            dpk[s, 128:256] = (dk * 0.125).astype(bf)
            dpk[s, 256:384] = dv.astype(bf)
            return carry

        lax.fori_loop(first_frame, first_frame + count, one, 0, unroll=True)

    @pl.when(t == 6)
    def _():
        def turn(f, s, sums):
            CB[f, 0] = oacc[s, :][:198].astype(bf)
            scaled, inverse = add_norm_stats(mid[s, :])
            grad = gsec[s, :]
            total = G[s, :].astype(f32) + norm_back(grad, scaled, inverse, gain2[...])
            gsec[s, :] = total
            sec[s, :] = total.astype(bf)
            oacc[s, :] = jnp.zeros((T, D), f32)
            return sums[0] + jnp.sum(grad * scaled, 0, keepdims=True), sums[1] + jnp.sum(grad, 0, keepdims=True)

        gg, gs = frames_loop(turn, (jnp.zeros((1, D), f32), jnp.zeros((1, D), f32)))
        SB[5:6, :] = gg
        SB[6:7, :] = gs
        AD[v_at * 8 + f_at] = pack_rows(SB[...])
        for send in small_near():
            send.start()
        fetch(4).start()
        fetch(3).start()
        for k in range(3):
            fetch(k).wait()
        G[0:RR, :] = dot(sec[0:RR, :], wo[...], 1, 1).astype(bf)

    @pl.when(t >= 6)
    def _():
        attend_back(0, 3)

    tick(2 * t)

    @pl.when(t < 6)
    def _():
        w_in, w_out = din(), dout()
        part = dot(sec[...], dinn[...], 0, 0)
        for q in range(4):
            for b in range(4):
                put(1, (q, b), part[q * ROWS : (q + 1) * ROWS, b * 128 : (b + 1) * 128])
        oacc[...] += dot(act[0:RR, 0:512], w_out)
        gsec[...] += dot(dinn[0:RR, :], w_in, 1, 1)

    @pl.when(t >= 6)
    def _():
        attend_back(3, 3)
        slot = lax.rem(head, 2)
        part = dot(first[...], dpk[...], 0, 0)
        for q in range(4):
            for b in range(3):
                put(slot, (q, b), part[q * ROWS : (q + 1) * ROWS, b * 128 : (b + 1) * 128])
        part = dot(mixed[...], sec[:, lanes], 0, 0)
        for q in range(4):
            put(slot, (q, 3), part[q * ROWS : (q + 1) * ROWS, :])

    tick(2 * t + 1)

    @pl.when(t >= 6)
    def _():
        w = jnp.concatenate([wq[...], wk[...], wv[...]], 1)
        oacc[...] += dot(dpk[0:RR, :], w, 1, 1)

    @pl.when(t == 8)
    def _():
        for k in (13, 14, 15):
            fetch(k).start()
        for send in small_near():
            send.wait()
        for send in small_far():
            send.start()

    @pl.when(t == STEPS - 1)
    def _():
        for k in (10, 11, 12):
            fetch(k).start()
        fetch(3).wait()
        last_row = lax.broadcasted_iota(jnp.int32, (16, D), 0) == 5

        def next_row(f, s, carry):
            s = pl.ds(pl.multiple_of(f * T + 192, 16), 16)
            values = jnp.where(last_row, mnext[pl.ds(f, 1), :], act[s, :].astype(f32))
            scaled, inverse = add_norm_stats(values)
            total = gsec[s, :] + norm_back(oacc[s, :], scaled, inverse, gain1[...])
            NB[pl.ds(f, 1), :] = total[5:6]
            return carry

        NB[...] = jnp.zeros((8, D), f32)
        frames_loop(next_row, 0)
        AN[v_at * 8 + f_at] = pack_rows(NB[...])
        for send in next_near():
            send.start()
        tick(24)

        def end(f, s, sums):
            values = act[s, :].astype(f32)
            low = jnp.where(last_row, mnext[pl.ds(f, 1), :], values[192:])
            scaled, inverse = add_norm_stats(jnp.concatenate([values[:192], low], 0))
            grad = oacc[s, :]
            total = gsec[s, :] + norm_back(grad, scaled, inverse, gain1[...])
            sec[s, :] = total.astype(bf)
            return sums[0] + jnp.sum(grad * scaled, 0, keepdims=True), sums[1] + jnp.sum(grad, 0, keepdims=True)

        gg, gs = frames_loop(end, (jnp.zeros((1, D), f32), jnp.zeros((1, D), f32)))
        fetch(5).start()
        NB[0:1, :] = gg
        NB[1:2, :] = gs
        AS[v_at * 8 + f_at] = pack_rows(NB[...])
        for send in sums_near():
            send.start()
        tick(25)
        tick(26)
        for send in next_near():
            send.wait()
        for send in next_far():
            send.start()
        for k in range(10, 16):
            fetch(k).wait()
        MS[...] = message_rows(unpack_rows(CLS[...]).astype(bf), G[0:D, :], mbias[...])
        scaled, _ = add_norm_stats(MS[...])
        LR[0] = (scaled * mgain[...] + mshift[...]).astype(bf)
        for o, ref in enumerate((first, mixed, mv)):
            MP[:, o * D : (o + 1) * D] = dot(LR[0], ref[0:D, :]).astype(bf)
        tick(28)
        for send in sums_near():
            send.wait()
        for send in sums_far():
            send.start()
        ik = lax.broadcasted_iota(jnp.int32, (MROWS, MROWS), 0)
        iq = lax.broadcasted_iota(jnp.int32, (MROWS, MROWS), 1)
        same = jnp.logical_and(lax.rem(ik, 8) == lax.rem(iq, 8), lax.div(ik, 64) == lax.div(iq, 64))
        mixed_rows, probs = attend_rows(MP[...], same, MROWS)
        LR[1] = mixed_rows
        for i, p in enumerate(probs):
            PR[i] = p
        tick(30)
        for send in next_far():
            send.wait()
        kind = lax.rem(lax.broadcasted_iota(jnp.int32, (MROWS, D), 0), 8)
        LR[2] = jnp.where(kind < 6, unpack_rows(AN[...]), 0.0).astype(bf)
        GM[...] = dot(LR[2], wo[...], 1, 1).astype(bf)
        rows_back(MP, PR, GM, GP, range(0, 3))
        tick(32)
        rows_back(MP, PR, GM, GP, range(3, 6))
        tick(34)
        grad = dot(GP[:, 0:D], first[0:D, :], 1, 1) + dot(GP[:, D : 2 * D], mixed[0:D, :], 1, 1)
        grad = grad + dot(GP[:, 2 * D : 3 * D], mv[...], 1, 1)
        scaled, inverse = add_norm_stats(MS[...])
        total = LR[2].astype(f32) + norm_back(grad, scaled, inverse, mgain[...])
        LR[3] = total.astype(bf)
        fetch(7).start()
        fetch(8).start()
        tick(36)
        HELD[...] = dot(LR[3], G[0:D, :], 1, 1)
        EDGE[0:8, :] = HELD[pl.ds(pl.multiple_of((v_at * 8 + f_at) * 8, 8), 8), :]
        lines = [jnp.sum(a, 0, keepdims=True) for a in (total, grad * scaled, grad)]
        for send in sums_far():
            send.wait()
        for send in small_far():
            send.wait()
        ends = jnp.sum(unpack_rows(AS[...]).reshape(32, 8, D), 0)
        small = jnp.sum(unpack_rows(AD[...]).reshape(32, 8, D), 0)
        lines += [ends[0:1], ends[1:2], small[5:6], small[6:7], small[4:5]]
        for i, line in enumerate(lines):
            EDGE[8 + i : 9 + i, :] = line
        EDGE[16:24, :] = small
        fetch(9).start()
        tick(38)

        def finish(g, carry):
            pltpu.make_async_copy(F.at[g], F_out.at[g], fsem.at[g]).wait()
            return carry

        lax.fori_loop(0, UNITS, finish, 0)
        for k in (4, 5, 7, 8, 9):
            fetch(k).wait()


def call_main(
    mid, cot, live, din, dout, bin_, bout, gain2, shift2, qkv, pt, wqkv, first, mixed, wo, tok, mnext, gain1,
    mproj, mqkv, mout, cls, mbias, mgain, mshift,
):
    one = pl.Buffered(1)
    full = lambda *s: pl.BlockSpec(s, lambda t: (0,) * len(s), pipeline_mode=one)
    hbm = pl.BlockSpec(memory_space=pl.ANY)
    dense = lambda t: jnp.minimum(t, 5)
    head = lambda t: jnp.maximum(t - 6, 0)
    specs = [full(RR, D), hbm, pl.BlockSpec(memory_space=pltpu.SMEM)]
    specs += [pl.BlockSpec((D, 128), lambda t, q=q: (0, q * 6 + dense(t))) for q in range(4)]
    specs += [pl.BlockSpec((128, D), lambda t, q=q: (q * 6 + dense(t), 0)) for q in range(4)]
    specs += [full(bin_.shape[0]), full(D), full(D), full(D)]
    specs += [pl.BlockSpec((1, RP, 384), lambda t: (head(t), 0, 0)), pl.BlockSpec((1, 12, T, T), lambda t: (head(t), 0, 0, 0))]
    specs += [pl.BlockSpec((D, 128), lambda t, o=o: (0, o * 6 + head(t))) for o in range(3)]
    specs += [hbm, hbm, hbm, hbm, full(8, D), full(D)] + [hbm] * 4 + [full(D)] * 3
    shape = jax.ShapeDtypeStruct
    dma = pltpu.SemaphoreType.DMA
    return pl.pallas_call(
        main_kernel,
        grid=(STEPS,),
        in_specs=specs,
        out_specs=[hbm] * 6,
        out_shape=[
            shape((FR, 1, 198, D), bf),
            shape((RR, D), bf),
            shape((UNITS, 4, ROWS, 128), bf),
            shape((MROWS, 3 * D), bf),
            shape((4, MROWS, D), bf),
            shape((24, D), f32),
        ],
        scratch_shapes=[
            pltpu.VMEM((RP, D), bf),
            pltpu.VMEM((RP, D), bf),
            pltpu.VMEM((RP, D), bf),
            pltpu.VMEM((RP, 512), bf),
            pltpu.VMEM((RR, D), f32),
            pltpu.VMEM((RR, D), f32),
            pltpu.VMEM((FR, 1, 198, D), bf),
            pltpu.VMEM((RP, D), bf),
            pltpu.VMEM((RP, D), bf),
            pltpu.VMEM((D, D), bf),
            pltpu.VMEM((RP, 384), bf),
            pltpu.VMEM((2, 2, 2, 4, ROWS, 128), bf),
            pltpu.VMEM((6, 2, 2, 2, ROWS, 128), bf),
            pltpu.VMEM((8, 2, 2, ROWS, 128), bf),
            pltpu.VMEM((8, 2, ROWS, 128), bf),
            pltpu.VMEM((UNITS, ROWS, 128), bf),
            pltpu.VMEM((UNITS, ROWS // 2, 128), bf),
            pltpu.VMEM((UNITS, 4, ROWS, 128), bf),
            pltpu.VMEM((1, 4 * D), f32),
            pltpu.VMEM((8, D), f32),
            pltpu.VMEM((8, D), f32),
            pltpu.VMEM((32, 16, D // 2), bf),
            pltpu.VMEM((32, 16, D // 2), bf),
            pltpu.VMEM((32, 16, D // 2), bf),
            pltpu.VMEM((D, D), bf),
            pltpu.VMEM((32, 16, D // 2), bf),
            pltpu.VMEM((MROWS, 3 * D), bf),
            pltpu.VMEM((12, MROWS, MROWS), bf),
            pltpu.VMEM((MROWS, D), f32),
            pltpu.VMEM((MROWS, 3 * D), bf),
            pltpu.VMEM((MROWS, D), bf),
            pltpu.VMEM((4, MROWS, D), bf),
            pltpu.VMEM((24, D), f32),
            pltpu.VMEM((MROWS, D), f32),
            dma((UNITS, 10)),
            dma((UNITS, 10)),
            dma((UNITS,)),
            dma((16,)),
            dma((10,)),
            dma((10,)),
            dma((10,)),
            dma((10,)),
            dma((10,)),
            dma((10,)),
        ],
        compiler_params=pltpu.CompilerParams(
            vmem_limit_bytes=VMEM_LIMIT,
            dimension_semantics=("arbitrary",),
            collective_id=1,
            has_side_effects=True,
        ),
    )(mid, cot, live, din, din, din, din, dout, dout, dout, dout, bin_, bout, gain2, shift2,
      qkv, pt, wqkv, wqkv, wqkv, first, mixed, wo, tok, mnext, gain1, mproj, mqkv, mout, cls, mbias, mgain, mshift)


def final_kernel(
    F, gt, cls_blocks, gpacked, lr, edge, out_in,
    out, gvid, gproj, gmqkv, gmout, gfqkv, gfout, gdin, gdout, *rest,
):
    vecs, bias_in = rest[:8], rest[8]
    v_at = lax.axis_index("video")
    out[...] = out_in[...]

    def pick(parts):
        return jnp.where(v_at == 0, parts[0], jnp.where(v_at == 1, parts[1], jnp.where(v_at == 2, parts[2], parts[3])))

    def mine(values):
        return pick([values[:, i * ROWS : (i + 1) * ROWS] for i in range(4)])

    gproj[...] = dot(mine(unpack_rows(cls_blocks[...]).astype(bf)), lr[3], 0, 0)
    gmqkv[...] = dot(mine(lr[0]), gpacked[...], 0, 0)
    gmout[...] = dot(mine(lr[1]), lr[2], 0, 0)
    picked = mine(edge[8:16, :])
    for i, ref in enumerate(vecs):
        ref[...] = picked[i]
    bias_in[...] = pick([edge[16 + i : 17 + i, :] for i in range(4)])[0]
    for f in range(FR):
        gvid[f, 0] = gt[f * T : (f + 1) * T, :][:197]
        gvid[f, 0, 0:1] = (gt[f * T : f * T + 16, :].astype(f32)[0:1] + edge[f : f + 1, :]).astype(bf)
    for j in range(6):
        for b in range(4):
            at = b * D + j * 128
            gdin[:, at : at + 128] = F[2 * j + 1, b].astype(f32)
            gdout[j * 128 : (j + 1) * 128, b * ROWS : (b + 1) * ROWS] = F[2 * j, b].astype(f32).T
            if b < 3:
                gfqkv[:, at : at + 128] = F[12 + j, b].astype(f32)
            else:
                gfout[:, j * 128 : (j + 1) * 128] = F[12 + j, b].astype(f32)


def call_final(F, gt, cls_blocks, gpacked, lr, edge, output):
    vm = pl.BlockSpec(memory_space=pltpu.VMEM)
    shape = jax.ShapeDtypeStruct
    return pl.pallas_call(
        final_kernel,
        in_specs=[vm] * 7,
        out_specs=[vm] * 18,
        out_shape=[
            shape((FR, 1, 198, D), bf),
            shape((FR, 1, 197, D), bf),
            shape((ROWS, D), f32),
            shape((ROWS, 3 * D), f32),
            shape((ROWS, D), f32),
            shape((ROWS, 3 * D), f32),
            shape((ROWS, D), f32),
            shape((ROWS, 4 * D), f32),
            shape((4 * ROWS, D), f32),
        ]
        + [shape((ROWS,), f32)] * 8
        + [shape((D,), f32)],
        compiler_params=pltpu.CompilerParams(vmem_limit_bytes=VMEM_LIMIT),
    )(F, gt, cls_blocks, gpacked, lr, edge, output)


def column_sum(values):
    return jnp.sum(values.reshape(-1, values.shape[-1]), axis=0)


def matmul(left, right):
    return jnp.dot(left, right, preferred_element_type=f32)


def back_matmul(grad_low, weight):
    return lax.dot_general(grad_low, weight, (((grad_low.ndim - 1,), (1,)), ((), ())), preferred_element_type=f32)


def weight_grad(inputs_low, grad_low):
    left = inputs_low.reshape(-1, inputs_low.shape[-1])
    right = grad_low.reshape(-1, grad_low.shape[-1])
    return lax.dot_general(left, right, (((0,), (0,)), ((), ())), preferred_element_type=f32)


def norm_forward(values, gain, shift):
    center = values - jnp.mean(values, axis=-1, keepdims=True)
    inverse = lax.rsqrt(jnp.mean(center * center, axis=-1, keepdims=True) + EPS)
    scaled = center * inverse
    return (scaled * gain + shift, scaled, inverse)


def norm_backward(grad_out, scaled, inverse, gain):
    grad_scaled = grad_out * gain
    grad_in = inverse * (
        grad_scaled
        - jnp.mean(grad_scaled, axis=-1, keepdims=True)
        - scaled * jnp.mean(grad_scaled * scaled, axis=-1, keepdims=True)
    )
    return (grad_in, column_sum(grad_out * scaled), column_sum(grad_out))


def split_heads(values):
    return values.reshape(values.shape[:-1] + (HEADS, HEAD_DIM))


def attend_forward(query_rows, key_rows, value_rows):
    scores = jnp.einsum("bqhd,bkhd->bhqk", query_rows, key_rows, preferred_element_type=f32) * 0.125
    largest = jnp.max(scores, axis=-1, keepdims=True)
    raised = jnp.exp(scores - largest)
    total = jnp.sum(raised, axis=-1, keepdims=True)
    probs_low = (raised / total).astype(bf)
    mixed = jnp.einsum("bhqk,bkhd->bqhd", probs_low, value_rows, preferred_element_type=f32)
    return (mixed, largest + jnp.log(total))


def attend_backward(query_rows, key_rows, value_rows, log_total, grad_mixed):
    scores = jnp.einsum("bqhd,bkhd->bhqk", query_rows, key_rows, preferred_element_type=f32) * 0.125
    probs = jnp.exp(scores - log_total)
    grad_probs = jnp.einsum("bqhd,bkhd->bhqk", grad_mixed, value_rows, preferred_element_type=f32)
    grad_scores = probs * (grad_probs - jnp.sum(grad_probs * probs, axis=-1, keepdims=True))
    grad_low = grad_scores.astype(bf)
    grad_query = jnp.einsum("bhqk,bkhd->bqhd", grad_low, key_rows, preferred_element_type=f32) * 0.125
    grad_key = jnp.einsum("bhqk,bqhd->bkhd", grad_low, query_rows, preferred_element_type=f32) * 0.125
    grad_value = jnp.einsum("bhqk,bqhd->bkhd", probs.astype(bf), grad_mixed, preferred_element_type=f32)
    return (grad_query, grad_key, grad_value)


def message_forward(video, message_proj, message_bias, message_gain, message_shift, message_qkv, message_out):
    width = video.shape[-1]
    batch, frames_local = video.shape[:2]
    class_rows = video[:, :, 0, :]
    message = (matmul(class_rows, message_proj) + message_bias).astype(bf)
    message_wide = message.astype(f32)
    normed_own, scaled_own, inverse_own = norm_forward(message_wide, message_gain, message_shift)
    normed_low = normed_own.astype(bf)
    everyone = lax.all_gather(message, "frame", axis=1, tiled=True)
    normed_all = norm_forward(everyone.astype(f32), message_gain, message_shift)[0]
    key_value = matmul(normed_all.astype(bf), message_qkv[:, width:]).astype(bf)
    query = split_heads(matmul(normed_low, message_qkv[:, :width]).astype(bf))
    key = split_heads(key_value[..., :width])
    value = split_heads(key_value[..., width:])
    mixed, total = attend_forward(query, key, value)
    mixed_low = mixed.reshape(batch, frames_local, width).astype(bf)
    message_next = message_wide + matmul(mixed_low, message_out)
    return message_next, (class_rows, normed_low, scaled_own, inverse_own, query, key, value, mixed_low, total)


def message_backward(kept, grad_next, message_proj, message_gain, message_qkv, message_out):
    class_rows, normed_low, scaled_own, inverse_own, query, key, value, mixed_low, total = kept
    batch, frames_local, width = grad_next.shape
    frames_all = key.shape[1]
    grad_next_low = grad_next.astype(bf)
    grad_mixed = split_heads(back_matmul(grad_next_low, message_out).astype(bf))
    grad_q, grad_k, grad_v = attend_backward(query, key, value, total, grad_mixed)
    key_value_grad = jnp.concatenate(
        [grad_k.reshape(batch, frames_all, width), grad_v.reshape(batch, frames_all, width)], axis=-1
    )
    own = lax.psum_scatter(key_value_grad.astype(bf), "frame", scatter_dimension=1, tiled=True)
    packed = jnp.concatenate([grad_q.reshape(batch, frames_local, width).astype(bf), own], axis=-1)
    grad_in, grad_gain, grad_shift = norm_backward(
        back_matmul(packed, message_qkv), scaled_own, inverse_own, message_gain
    )
    grad_message = grad_next + grad_in
    grad_message_low = grad_message.astype(bf)
    grad_class = back_matmul(grad_message_low, message_proj)
    rows = jnp.concatenate([class_rows, normed_low, mixed_low, grad_message_low, packed, grad_next_low], axis=-1)
    rows = rows.reshape(batch * frames_local, -1)
    return grad_class, rows, column_sum(grad_message), grad_gain, grad_shift


def reduced_inside(
    video, video_live, cotangent, message_proj, message_bias, message_gain, message_shift, message_qkv,
    message_out, frame_gain, frame_shift, frame_qkv, frame_out, dense_gain, dense_shift, dense_in,
    dense_in_bias, dense_out, dense_out_bias,
):
    packed, probs, first, mixed, middle, tokens, next_rows, class_blocks = call_first(
        video, frame_qkv, frame_out, frame_gain, frame_shift,
        message_proj, message_bias, message_gain, message_shift, message_qkv, message_out,
    )
    output, grad_rows, reduced, grad_packed, sides, edge = call_main(
        middle, cotangent, video_live, dense_in, dense_out, dense_in_bias, dense_out_bias, dense_gain, dense_shift,
        packed, probs, frame_qkv, first, mixed, frame_out, tokens, next_rows, frame_gain,
        message_proj, message_qkv, message_out, class_blocks, message_bias, message_gain, message_shift,
    )
    output, grad_input, g_proj, g_mqkv, g_mout, g_fqkv, g_fout, g_in, g_out, *lines = call_final(
        reduced, grad_rows, class_blocks, grad_packed, sides, edge, output
    )
    return (
        output, grad_input, g_proj, lines[0], lines[1], lines[2], g_mqkv, g_mout, lines[3], lines[4], g_fqkv, g_fout,
        lines[5], lines[6], g_in, lines[8], g_out, lines[7],
    )


def local(
    video,
    video_live,
    cotangent,
    message_proj,
    message_bias,
    message_gain,
    message_shift,
    message_qkv,
    message_out,
    frame_gain,
    frame_shift,
    frame_qkv,
    frame_out,
    dense_gain,
    dense_shift,
    dense_in,
    dense_in_bias,
    dense_out,
    dense_out_bias,
):
    batch, frames_local, patches, width = video.shape
    hidden = dense_in.shape[1]
    groups = lax.axis_size("video")
    if (lax.axis_size("frame"), groups) == (8, 4):
        return reduced_inside(
            video, video_live, cotangent, message_proj, message_bias, message_gain, message_shift, message_qkv,
            message_out, frame_gain, frame_shift, frame_qkv, frame_out, dense_gain, dense_shift, dense_in,
            dense_in_bias, dense_out, dense_out_bias,
        )
    message_next, kept = message_forward(
        video, message_proj, message_bias, message_gain, message_shift, message_qkv, message_out
    )
    next_rows = message_next.reshape(batch * frames_local, width)
    packed, probs, first, mixed, middle, _ = call_k1(video, next_rows, frame_qkv, frame_out, frame_gain, frame_shift)
    output, grad_middle, part_in, part_out, part_bias, dense_small = call_k2(
        middle, cotangent, video_live, dense_in, dense_out, dense_in_bias, dense_out_bias, dense_gain, dense_shift
    )
    grad_tokens, part_frame, frame_small = call_k3(
        video, next_rows, grad_middle, packed, probs, first, mixed, frame_qkv, frame_out, frame_gain
    )
    grad_tokens = grad_tokens.reshape(batch, frames_local, T, width)
    grad_next = grad_tokens[:, :, patches]
    grad_class, rows, sum_bias, sum_gain, sum_shift = message_backward(
        kept, grad_next, message_proj, message_gain, message_qkv, message_out
    )
    grad_input = jnp.concatenate(
        [grad_tokens[:, :, :1] + grad_class[:, :, None, :], grad_tokens[:, :, 1:patches]], axis=2
    ).astype(bf)

    def total(value):
        share = lax.psum_scatter(value, "video", scatter_dimension=0, tiled=True)
        return lax.psum(share, "frame").astype(f32)

    grad_in = total(part_in.reshape(6, width, 4, 128).transpose(1, 2, 0, 3).reshape(width, hidden))
    grad_out = total(part_out.reshape(6, width, 4, 128).transpose(2, 0, 3, 1).reshape(hidden, width))
    part_frame = part_frame.reshape(6, width, 4, 128).transpose(1, 2, 0, 3).reshape(width, 4 * width)
    grad_frame = total(part_frame)
    vector = jnp.concatenate(
        [
            sum_bias,
            sum_gain,
            sum_shift,
            frame_small[0],
            frame_small[1],
            dense_small[1],
            dense_small[2],
            dense_small[0],
            part_bias.reshape(6, 4, 128).transpose(1, 0, 2).reshape(hidden),
        ]
    )
    vector = lax.psum(vector, ("video", "frame"))
    place = lax.axis_index("video")
    cut = width // groups

    def mine(start, length):
        return lax.dynamic_slice_in_dim(vector, start + place * (length // groups), length // groups)

    gathered = lax.all_gather(rows, ("video", "frame"), axis=0, tiled=True)

    def outer(left, first_column, last_column):
        part = lax.dynamic_slice_in_dim(gathered, left * width + place * cut, cut, axis=1)
        return weight_grad(part, gathered[:, first_column:last_column])

    return (
        output,
        grad_input,
        outer(0, 3 * width, 4 * width),
        mine(0, width),
        mine(width, width),
        mine(2 * width, width),
        outer(1, 4 * width, 7 * width),
        outer(2, 7 * width, 8 * width),
        mine(3 * width, width),
        mine(4 * width, width),
        grad_frame[:, : 3 * width],
        grad_frame[:, 3 * width :],
        mine(5 * width, width),
        mine(6 * width, width),
        grad_in,
        mine(8 * width, hidden),
        grad_out,
        mine(7 * width, width),
    )


def solution(mesh):
    in_specs = (
        P("video", "frame", None, None),
        P("video"),
        P("video", "frame", None, None),
        P(),
        P(),
        P(),
        P(),
        P(),
        P(),
        P(),
        P(),
        P(),
        P(),
        P(),
        P(),
        P(),
        P(),
        P(),
        P(),
    )
    out_specs = (
        P("video", "frame", None, None),
        P("video", "frame", None, None),
        P("video", None),
        P("video"),
        P("video"),
        P("video"),
        P("video", None),
        P("video", None),
        P("video"),
        P("video"),
        P("video", None),
        P("video", None),
        P("video"),
        P("video"),
        P("video", None),
        P("video"),
        P("video", None),
        P("video"),
    )
    return jax.shard_map(local, mesh=mesh, in_specs=in_specs, out_specs=out_specs, check_vma=False)
```

profile of v0, /device:TPU:0, one launch (start us, length us, event | category | flops | bytes accessed | tf_op | source)
XLA Modules:
  0.0 183.6 jit_solution(14453809474027549338)
XLA Ops:
  0.7 43.8 %shard_map.322 = (bf16[6,1280,384]{2,1,0:T(8,128)(2,1)}, bf16[6,12,208,208]{3,2,1,0:T(8,128)(2,1)}, bf16[1280,768]{1,0:T(8,128)(2,1)}, bf16[1280,768]{1,0:T(8,12...) custom-call(bf16[6,1,197,768]{3,2,1,0:T(8,128)(2,1)} %vid.1, ...), custom_call_target="tpu_custom_call" | custom-call | tf_op jit(solution)/shard_map/pallas_call | solution.py:393
  44.5 128.6 %shard_map.323 = (bf16[6,1,198,768]{3,2,1,0:T(8,128)(2,1)}, bf16[1248,768]{1,0:T(8,128)(2,1)}, bf16[18,4,192,128]{3,2,1,0:T(8,128)(2,1)}, bf16[256,2304]{1,0:T(8...) custom-call(f32[1248,768]{1,0:T(8,128)} %get-tuple-element.50.mid, bf16[6,1,198,768]{3,2,1,0:T(8,128)(2,1)} %cot.1, ...), custom_call_target="tpu_custom_call" | custom-call | tf_op jit(solution)/shard_map/pallas_call | solution.py:907
  173.0 10.3 %shard_map.324 = (bf16[6,1,198,768]{3,2,1,0:T(8,128)(2,1)}, bf16[6,1,197,768]{3,2,1,0:T(8,128)(2,1)}, f32[192,768]{1,0:T(8,128)}, f32[192,2304]{1,0:T(8,128)}, f...) custom-call(bf16[18,4,192,128]{3,2,1,0:T(8,128)(2,1)} %get-tuple-ele, ...), custom_call_target="tpu_custom_call" | custom-call | tf_op jit(solution)/shard_map/pallas_call | solution.py:1014
where the time goes:
time: 184 us
  Pallas kernels  183 us (99%)
    pallas_call x1, Pallas kernels, call_main(): pl.pallas_call(main_kernel, grid=(STEPS,), in_specs=specs, out_specs=[hbm...  129 us
    pallas_call x1, Pallas kernels, call_first(): pl.pallas_call(first_kernel, grid=(6,), in_specs=specs, out_specs=[blk(RP...  43.8 us
    pallas_call x1, Pallas kernels, call_final(): pl.pallas_call(final_kernel, in_specs=[vm] * 7, out_specs=[vm] * 18, out_...  10.3 us

commit v1 on v0

--- a/solution.py
+++ b/solution.py
@@ -308,8 +308,8 @@
 
 def first_kernel(
     vid, wq, wk, wv, wo, gain, shift, mproj_h, mqkv_h, mout_h, mbias, mgain, mshift,
-    qkv_ref, pt_ref, first_ref, mixed_ref, mid_ref, tok_ref, mnext_ref, cls_ref,
-    mproj, mqkv, mout, B, mrows, wsem, ssem, rsem,
+    qkv_ref, pt_ref, first_out, mixed_ref, mid_ref, tok_out, mnext_ref, cls_ref,
+    mproj, mqkv, mout, B, mrows, FI, TK, MX, wsem, ssem, rsem, osem,
 ):
     h = pl.program_id(0)
     f_at, v_at = lax.axis_index("frame"), lax.axis_index("video")
@@ -317,8 +317,8 @@
 
     def put_rows(rows, values):
         scaled, _ = add_norm_stats(values)
-        first_ref[rows, :] = (scaled * gain[...] + shift[...]).astype(bf)
-        tok_ref[rows, :] = values.astype(bf)
+        FI[rows, :] = (scaled * gain[...] + shift[...]).astype(bf)
+        TK[rows, :] = values.astype(bf)
 
     @pl.when(h == 0)
     def _():
@@ -335,8 +335,8 @@
         sends = near()
         for send in sends:
             send.start()
-        first_ref[pl.ds(RR, RP - RR), :] = jnp.zeros((RP - RR, D), bf)
-        mixed_ref[pl.ds(RR, RP - RR), :] = jnp.zeros((RP - RR, D), bf)
+        FI[pl.ds(RR, RP - RR), :] = jnp.zeros((RP - RR, D), bf)
+        MX[pl.ds(RR, RP - RR), :] = jnp.zeros((RP - RR, D), bf)
         def begin(f, rows, carry):
             mid_ref[rows, :] = jnp.concatenate([vid[f, 0].astype(f32), jnp.zeros((T - 197, D), f32)], 0)
             rows = pl.ds(pl.multiple_of(f * T, 16), 192)
@@ -371,10 +371,20 @@
 
         frames_loop(finish, 0)
 
-    attend_frames(h, wq, wk, wv, wo, qkv_ref, pt_ref, first_ref, mixed_ref, mid_ref)
+    keeps = [pltpu.make_async_copy(src, dst, osem.at[i]) for i, (src, dst) in enumerate(((FI, first_out), (TK, tok_out)))]
+
+    @pl.when(h == 0)
+    def _():
+        for copy in keeps:
+            copy.start()
+
+    attend_frames(h, wq, wk, wv, wo, qkv_ref, pt_ref, FI, MX, mid_ref)
+    mixed_ref[...] = MX[:, pl.ds(pl.multiple_of(h * 128, 128), 128)]
 
     @pl.when(h == 5)
     def _():
+        for copy in keeps:
+            copy.wait()
         for send in far():
             send.wait()
         cls_ref[...] = B[...]
@@ -395,7 +405,7 @@
         grid=(6,),
         in_specs=specs,
         out_specs=[
-            blk(RP, 384), blk(12, T, T), keep(RP, D), keep(RP, D), keep(RR, D), keep(RR, D), keep(8, D),
+            blk(RP, 384), blk(12, T, T), hbm, pl.BlockSpec((RP, 128), lambda j: (0, j)), keep(RR, D), hbm, keep(8, D),
             keep(32, 16, D // 2),
         ],
         out_shape=[
@@ -414,9 +424,13 @@
             pltpu.VMEM((D, D), bf),
             pltpu.VMEM((32, 16, D // 2), bf),
             pltpu.VMEM((64, D), f32),
+            pltpu.VMEM((RP, D), bf),
+            pltpu.VMEM((RR, D), bf),
+            pltpu.VMEM((RP, D), bf),
             dma((3,)),
             dma((10,)),
             dma((10,)),
+            dma((2,)),
         ],
         compiler_params=pltpu.CompilerParams(
             vmem_limit_bytes=VMEM_LIMIT, dimension_semantics=("arbitrary",), collective_id=2, has_side_effects=True
@@ -427,12 +441,40 @@
 MROWS = 256
 
 
-def rows_back(MP, PR, GM, GP, heads):
+def rows_forward(MP, PR, out):
     lo = lax.broadcasted_iota(jnp.int32, (MROWS, 128), 1) < 64
     zero = jnp.zeros((MROWS, 128), bf)
-    for h in heads:
-        q, k, v = (MP[:, o * D + h * 128 : o * D + (h + 1) * 128] for o in range(3))
-        do = GM[:, h * 128 : (h + 1) * 128]
+    ik = lax.broadcasted_iota(jnp.int32, (MROWS, MROWS), 0)
+    iq = lax.broadcasted_iota(jnp.int32, (MROWS, MROWS), 1)
+    same = jnp.logical_and(lax.rem(ik, 8) == lax.rem(iq, 8), lax.div(ik, 64) == lax.div(iq, 64))
+
+    def one(h, carry):
+        lanes = lambda o: pl.ds(pl.multiple_of(o * D + h * 128, 128), 128)
+        q, k, v = (MP[:, lanes(o)] for o in range(3))
+        q = q * jnp.asarray(0.125, bf)
+        ps, vs = [], []
+        for e in range(2):
+            m = lo if e == 0 else jnp.logical_not(lo)
+            st = jnp.where(same, dot(k, jnp.where(m, q, zero), 1, 1), NEG)
+            raised = jnp.exp(st - jnp.max(st, 0, keepdims=True))
+            p = (raised * (1.0 / jnp.sum(raised, 0, keepdims=True))).astype(bf)
+            PR[2 * h + e] = p
+            ps.append(p)
+            vs.append(jnp.where(m, v, zero))
+        out[1, :, lanes(0)] = dot(jnp.concatenate(ps, 0), jnp.concatenate(vs, 0), 0, 0).astype(bf)
+        return carry
+
+    lax.fori_loop(0, 6, one, 0)
+
+
+def rows_back(MP, PR, GM, GP, start):
+    lo = lax.broadcasted_iota(jnp.int32, (MROWS, 128), 1) < 64
+    zero = jnp.zeros((MROWS, 128), bf)
+
+    def one(h, carry):
+        lanes = lambda o: pl.ds(pl.multiple_of(o * D + h * 128, 128), 128)
+        q, k, v = (MP[:, lanes(o)] for o in range(3))
+        do = GM[:, lanes(0)]
         dss, ks, dk, dv = [], [], 0.0, 0.0
         for e in range(2):
             m = lo if e == 0 else jnp.logical_not(lo)
@@ -447,7 +489,10 @@
             ks.append(jnp.where(m, k, zero))
         dq = dot(jnp.concatenate(dss, 0), jnp.concatenate(ks, 0), 0, 0) * 0.125
         for o, part in enumerate((dq, dk * 0.125, dv)):
-            GP[:, o * D + h * 128 : o * D + (h + 1) * 128] = part.astype(bf)
+            GP[:, lanes(o)] = part.astype(bf)
+        return carry
+
+    lax.fori_loop(start, start + 3, one, 0)
 
 
 def frames_loop(body, carry):
@@ -457,23 +502,29 @@
     return lax.fori_loop(0, FR, step, carry)
 
 
-def exchange(tick, where, U, RA, RB, RC, RD, RE, F, ssem, rsem, fsem, F_out):
+def exchange(tick, odd, where, U, RA, RB, RC, RD, RE, F, ssem, rsem, fsem, F_out):
     c, x, y, z0, z1, core, xn, yn, zn, zf = where
 
-    def at(lag_dense, lag_frame, body):
-        dense = tick - lag_dense
-        late = tick - lag_frame - 13
-        step = lax.div(jnp.maximum(late, 0), 2)
-        is_dense = jnp.logical_and(dense >= 0, dense < 12)
-        is_frame = jnp.logical_and(jnp.logical_and(late >= 0, lax.rem(jnp.maximum(late, 0), 2) == 0), step < 6)
-
-        @pl.when(is_dense)
+    def at(lag, body):
+        if isinstance(tick, int):
+            late = tick - lag
+            if 0 <= late < 12:
+                body(late)
+            if 0 <= late - 13 <= 10 and late % 2 == 1:
+                body(12 + (late - 13) // 2)
+            return
+        dense = tick - lag
+
+        @pl.when(jnp.logical_and(dense >= 0, dense < 12))
         def _():
             body(jnp.clip(dense, 0, 11))
 
-        @pl.when(is_frame)
-        def _():
-            body(12 + jnp.minimum(step, 5))
+        if (lag + odd) % 2:
+            late = tick - lag - 13
+
+            @pl.when(late >= 0)
+            def _():
+                body(12 + lax.div(jnp.maximum(late, 0), 2))
 
     def move(g, k, src, dst, target):
         return pltpu.make_async_remote_copy(
@@ -567,16 +618,16 @@
 
     bodies = (on_a, on_b, on_c, on_d1, on_d2, on_e2, on_e1, on_last, on_done)
     for lag, body in zip(LAG, bodies):
-        at(lag, lag, body)
+        at(lag, body)
 
 
 def main_kernel(
     mid, cot, live, din0, din1, din2, din3, do0, do1, do2, do3, bin_, bout, gain2, shift2,
-    qkv, pt, wq, wk, wv, first_hbm, mixed_hbm, wo_hbm, tok_hbm, mnext, gain1,
+    qkv, pt, wqkv_hbm, first_hbm, mixed_hbm, wo_hbm, tok_hbm, mnext, gain1,
     mproj_hbm, mqkv_hbm, mout_hbm, cls_hbm, mbias, mgain, mshift,
     out_hbm, gt_hbm, F_out, gp_out, lr_out, edge_out,
     sec, G, act, dinn, oacc, gsec, CB, first, mixed, wo, dpk,
-    U, RA, RB, RC, RD, RE, F, BI, SB, NB, AD, AN, AS, mv, CLS, MP, PR, MS, GP, GM, LR, EDGE, HELD, ssem, rsem, fsem, lsem, adsem, adrem, ansem, anrem, assem, asrem,
+    U, RA, RB, RC, RD, RE, F, BI, SB, NB, AD, AN, AS, WQ, CLS, MP, PR, GP, GM, LR, EDGE, ssem, rsem, fsem, lsem, adsem, adrem, ansem, anrem, assem, asrem,
 ):
     t = pl.program_id(0)
     f_at, v_at = lax.axis_index("frame"), lax.axis_index("video")
@@ -594,8 +645,8 @@
     next_near, next_far = gather_moves(AN, ansem, anrem, f_at, v_at)
     sums_near, sums_far = gather_moves(AS, assem, asrem, f_at, v_at)
 
-    def tick(n):
-        exchange(n, where, U, RA, RB, RC, RD, RE, F, ssem, rsem, fsem, F_out)
+    def tick(n, odd=0):
+        exchange(n, odd, where, U, RA, RB, RC, RD, RE, F, ssem, rsem, fsem, F_out)
 
     def fetch(k):
         src, dst = (
@@ -612,9 +663,10 @@
             (mproj_hbm, G.at[pl.ds(0, D)]),
             (mqkv_hbm.at[:, pl.ds(0, D)], first.at[pl.ds(0, D)]),
             (mqkv_hbm.at[:, pl.ds(D, D)], mixed.at[pl.ds(0, D)]),
-            (mqkv_hbm.at[:, pl.ds(2 * D, D)], mv),
+            (mqkv_hbm.at[:, pl.ds(2 * D, D)], act.at[pl.ds(0, D)]),
             (mout_hbm, wo),
             (cls_hbm, CLS),
+            (wqkv_hbm, WQ),
         )[k]
         return pltpu.make_async_copy(src, dst, lsem.at[k])
 
@@ -630,7 +682,7 @@
         G[tail, :] = jnp.zeros((RP - RR, D), bf)
         act[tail, :] = jnp.zeros((RP - RR, D), bf)
         dinn[tail, :] = jnp.zeros((RP - RR, 512), bf)
-        dpk[tail, :] = jnp.zeros((RP - RR, 384), bf)
+        dpk[tail, :] = jnp.zeros((RP - RR, 3 * D), bf)
         SB[...] = jnp.zeros((8, D), f32)
         BI[...] = bin_[...].reshape(1, 4 * D)
         def begin(f, rows, carry):
@@ -686,6 +738,7 @@
     zero = jnp.zeros((T, 128), bf)
     head = jnp.maximum(t - 6, 0)
     lanes = pl.ds(pl.multiple_of(head * 128, 128), 128)
+    third = lambda o: pl.ds(pl.multiple_of(o * D + head * 128, 128), 128)
 
     def attend_back(first_frame, count):
         def one(f, carry):
@@ -705,9 +758,8 @@
                 dss.append(ds)
                 ks.append(jnp.where(m, k, zero))
             dq = dot(jnp.concatenate(dss, 0), jnp.concatenate(ks, 0), 0, 0) * 0.125
-            dpk[s, 0:128] = dq.astype(bf)
-            dpk[s, 128:256] = (dk * 0.125).astype(bf)
-            dpk[s, 256:384] = dv.astype(bf)
+            for o, part in enumerate((dq, dk * 0.125, dv)):
+                dpk[s, third(o)] = part.astype(bf)
             return carry
 
         lax.fori_loop(first_frame, first_frame + count, one, 0, unroll=True)
@@ -721,7 +773,6 @@
             total = G[s, :].astype(f32) + norm_back(grad, scaled, inverse, gain2[...])
             gsec[s, :] = total
             sec[s, :] = total.astype(bf)
-            oacc[s, :] = jnp.zeros((T, D), f32)
             return sums[0] + jnp.sum(grad * scaled, 0, keepdims=True), sums[1] + jnp.sum(grad, 0, keepdims=True)
 
         gg, gs = frames_loop(turn, (jnp.zeros((1, D), f32), jnp.zeros((1, D), f32)))
@@ -756,7 +807,7 @@
     def _():
         attend_back(3, 3)
         slot = lax.rem(head, 2)
-        part = dot(first[...], dpk[...], 0, 0)
+        part = dot(first[...], jnp.concatenate([dpk[:, third(o)] for o in range(3)], 1), 0, 0)
         for q in range(4):
             for b in range(3):
                 put(slot, (q, b), part[q * ROWS : (q + 1) * ROWS, b * 128 : (b + 1) * 128])
@@ -764,16 +815,11 @@
         for q in range(4):
             put(slot, (q, 3), part[q * ROWS : (q + 1) * ROWS, :])
 
-    tick(2 * t + 1)
-
-    @pl.when(t >= 6)
-    def _():
-        w = jnp.concatenate([wq[...], wk[...], wv[...]], 1)
-        oacc[...] += dot(dpk[0:RR, :], w, 1, 1)
+    tick(2 * t + 1, 1)
 
     @pl.when(t == 8)
     def _():
-        for k in (13, 14, 15):
+        for k in (14, 15, 16):
             fetch(k).start()
         for send in small_near():
             send.wait()
@@ -787,20 +833,32 @@
         fetch(3).wait()
         last_row = lax.broadcasted_iota(jnp.int32, (16, D), 0) == 5
 
-        def next_row(f, s, carry):
-            s = pl.ds(pl.multiple_of(f * T + 192, 16), 16)
-            values = jnp.where(last_row, mnext[pl.ds(f, 1), :], act[s, :].astype(f32))
+        fetch(16).wait()
+        grads = dot(jnp.concatenate([dpk[f * T + 192 : (f + 1) * T, :] for f in range(FR)], 0), WQ[...], 1, 1)
+        NB[...] = jnp.zeros((8, D), f32)
+        for f in range(FR):
+            s = slice(f * T + 192, (f + 1) * T)
+            values = jnp.where(last_row, mnext[f : f + 1, :], act[s, :].astype(f32))
             scaled, inverse = add_norm_stats(values)
-            total = gsec[s, :] + norm_back(oacc[s, :], scaled, inverse, gain1[...])
-            NB[pl.ds(f, 1), :] = total[5:6]
-            return carry
-
-        NB[...] = jnp.zeros((8, D), f32)
-        frames_loop(next_row, 0)
+            total = gsec[s, :] + norm_back(grads[16 * f : 16 * f + 16], scaled, inverse, gain1[...])
+            NB[f : f + 1, :] = total[5:6]
         AN[v_at * 8 + f_at] = pack_rows(NB[...])
         for send in next_near():
             send.start()
         tick(24)
+
+        def widen(r, carry):
+            s = pl.ds(pl.multiple_of(r * 416, 16), 416)
+            oacc[s, :] = dot(dpk[s, :], WQ[...], 1, 1)
+            return carry
+
+        lax.fori_loop(0, 3, widen, 0)
+        tick(25)
+        tick(26)
+        for send in next_near():
+            send.wait()
+        for send in next_far():
+            send.start()
 
         def end(f, s, sums):
             values = act[s, :].astype(f32)
@@ -813,56 +871,46 @@
 
         gg, gs = frames_loop(end, (jnp.zeros((1, D), f32), jnp.zeros((1, D), f32)))
         fetch(5).start()
+        fetch(13).start()
         NB[0:1, :] = gg
         NB[1:2, :] = gs
         AS[v_at * 8 + f_at] = pack_rows(NB[...])
         for send in sums_near():
             send.start()
-        tick(25)
-        tick(26)
-        for send in next_near():
-            send.wait()
-        for send in next_far():
-            send.start()
-        for k in range(10, 16):
+        tick(28)
+        for k in (10, 11, 12, 14, 15):
             fetch(k).wait()
-        MS[...] = message_rows(unpack_rows(CLS[...]).astype(bf), G[0:D, :], mbias[...])
-        scaled, _ = add_norm_stats(MS[...])
+        gsec[0:MROWS, :] = message_rows(unpack_rows(CLS[...]).astype(bf), G[0:D, :], mbias[...])
+        scaled, _ = add_norm_stats(gsec[0:MROWS, :])
         LR[0] = (scaled * mgain[...] + mshift[...]).astype(bf)
-        for o, ref in enumerate((first, mixed, mv)):
+        fetch(13).wait()
+        for o, ref in enumerate((first, mixed, act)):
             MP[:, o * D : (o + 1) * D] = dot(LR[0], ref[0:D, :]).astype(bf)
-        tick(28)
+        tick(30)
         for send in sums_near():
             send.wait()
         for send in sums_far():
             send.start()
-        ik = lax.broadcasted_iota(jnp.int32, (MROWS, MROWS), 0)
-        iq = lax.broadcasted_iota(jnp.int32, (MROWS, MROWS), 1)
-        same = jnp.logical_and(lax.rem(ik, 8) == lax.rem(iq, 8), lax.div(ik, 64) == lax.div(iq, 64))
-        mixed_rows, probs = attend_rows(MP[...], same, MROWS)
-        LR[1] = mixed_rows
-        for i, p in enumerate(probs):
-            PR[i] = p
-        tick(30)
+        rows_forward(MP, PR, LR)
+        tick(32)
         for send in next_far():
             send.wait()
         kind = lax.rem(lax.broadcasted_iota(jnp.int32, (MROWS, D), 0), 8)
         LR[2] = jnp.where(kind < 6, unpack_rows(AN[...]), 0.0).astype(bf)
         GM[...] = dot(LR[2], wo[...], 1, 1).astype(bf)
-        rows_back(MP, PR, GM, GP, range(0, 3))
-        tick(32)
-        rows_back(MP, PR, GM, GP, range(3, 6))
+        rows_back(MP, PR, GM, GP, 0)
         tick(34)
+        rows_back(MP, PR, GM, GP, 3)
         grad = dot(GP[:, 0:D], first[0:D, :], 1, 1) + dot(GP[:, D : 2 * D], mixed[0:D, :], 1, 1)
-        grad = grad + dot(GP[:, 2 * D : 3 * D], mv[...], 1, 1)
-        scaled, inverse = add_norm_stats(MS[...])
+        grad = grad + dot(GP[:, 2 * D : 3 * D], act[0:D, :], 1, 1)
+        scaled, inverse = add_norm_stats(gsec[0:MROWS, :])
         total = LR[2].astype(f32) + norm_back(grad, scaled, inverse, mgain[...])
         LR[3] = total.astype(bf)
         fetch(7).start()
         fetch(8).start()
         tick(36)
-        HELD[...] = dot(LR[3], G[0:D, :], 1, 1)
-        EDGE[0:8, :] = HELD[pl.ds(pl.multiple_of((v_at * 8 + f_at) * 8, 8), 8), :]
+        oacc[0:MROWS, :] = dot(LR[3], G[0:D, :], 1, 1)
+        EDGE[0:8, :] = oacc[pl.ds(pl.multiple_of((v_at * 8 + f_at) * 8, 8), 8), :]
         lines = [jnp.sum(a, 0, keepdims=True) for a in (total, grad * scaled, grad)]
         for send in sums_far():
             send.wait()
@@ -900,8 +948,7 @@
     specs += [pl.BlockSpec((128, D), lambda t, q=q: (q * 6 + dense(t), 0)) for q in range(4)]
     specs += [full(bin_.shape[0]), full(D), full(D), full(D)]
     specs += [pl.BlockSpec((1, RP, 384), lambda t: (head(t), 0, 0)), pl.BlockSpec((1, 12, T, T), lambda t: (head(t), 0, 0, 0))]
-    specs += [pl.BlockSpec((D, 128), lambda t, o=o: (0, o * 6 + head(t))) for o in range(3)]
-    specs += [hbm, hbm, hbm, hbm, full(8, D), full(D)] + [hbm] * 4 + [full(D)] * 3
+    specs += [hbm, hbm, hbm, hbm, hbm, full(8, D), full(D)] + [hbm] * 4 + [full(D)] * 3
     shape = jax.ShapeDtypeStruct
     dma = pltpu.SemaphoreType.DMA
     return pl.pallas_call(
@@ -928,7 +975,7 @@
             pltpu.VMEM((RP, D), bf),
             pltpu.VMEM((RP, D), bf),
             pltpu.VMEM((D, D), bf),
-            pltpu.VMEM((RP, 384), bf),
+            pltpu.VMEM((RP, 3 * D), bf),
             pltpu.VMEM((2, 2, 2, 4, ROWS, 128), bf),
             pltpu.VMEM((6, 2, 2, 2, ROWS, 128), bf),
             pltpu.VMEM((8, 2, 2, ROWS, 128), bf),
@@ -942,20 +989,18 @@
             pltpu.VMEM((32, 16, D // 2), bf),
             pltpu.VMEM((32, 16, D // 2), bf),
             pltpu.VMEM((32, 16, D // 2), bf),
-            pltpu.VMEM((D, D), bf),
+            pltpu.VMEM((D, 3 * D), bf),
             pltpu.VMEM((32, 16, D // 2), bf),
             pltpu.VMEM((MROWS, 3 * D), bf),
             pltpu.VMEM((12, MROWS, MROWS), bf),
-            pltpu.VMEM((MROWS, D), f32),
             pltpu.VMEM((MROWS, 3 * D), bf),
             pltpu.VMEM((MROWS, D), bf),
             pltpu.VMEM((4, MROWS, D), bf),
             pltpu.VMEM((24, D), f32),
-            pltpu.VMEM((MROWS, D), f32),
             dma((UNITS, 10)),
             dma((UNITS, 10)),
             dma((UNITS,)),
-            dma((16,)),
+            dma((17,)),
             dma((10,)),
             dma((10,)),
             dma((10,)),
@@ -970,7 +1015,7 @@
             has_side_effects=True,
         ),
     )(mid, cot, live, din, din, din, din, dout, dout, dout, dout, bin_, bout, gain2, shift2,
-      qkv, pt, wqkv, wqkv, wqkv, first, mixed, wo, tok, mnext, gain1, mproj, mqkv, mout, cls, mbias, mgain, mshift)
+      qkv, pt, wqkv, first, mixed, wo, tok, mnext, gain1, mproj, mqkv, mout, cls, mbias, mgain, mshift)
 
 
 def final_kernel(

time: 184 us -> 179 us (0.973)
  Pallas kernels: 183 us -> 178 us
    pallas_call x1, Pallas kernels: 129 us -> 125 us  [call_main(): pl.pallas_call(main_kernel, grid=(STEPS,), in_specs=specs, out_specs=[hbm...]
where the time goes in v1:
time: 179 us
  Pallas kernels  178 us (99%)
    pallas_call x1, Pallas kernels, call_main(): pl.pallas_call(main_kernel, grid=(STEPS,), in_specs=specs, out_specs=[hbm...  125 us
    pallas_call x1, Pallas kernels, call_first(): pl.pallas_call(first_kernel, grid=(6,), in_specs=specs, out_specs=[blk(RP...  42.6 us
    pallas_call x1, Pallas kernels, call_final(): pl.pallas_call(final_kernel, in_specs=[vm] * 7, out_specs=[vm] * 18, out_...  10.3 us

profile of v1, /device:TPU:0, one launch (start us, length us, event | category | flops | bytes accessed | tf_op | source)
XLA Modules:
  0.0 178.9 jit_solution(5296145441948188009)
XLA Ops:
  0.7 42.6 %shard_map.322 = (bf16[6,1280,384]{2,1,0:T(8,128)(2,1)}, bf16[6,12,208,208]{3,2,1,0:T(8,128)(2,1)}, bf16[1280,768]{1,0:T(8,128)(2,1)}, bf16[1280,768]{1,0:T(8,12...) custom-call(bf16[6,1,197,768]{3,2,1,0:T(8,128)(2,1)} %vid.1, ...), custom_call_target="tpu_custom_call" | custom-call | tf_op jit(solution)/shard_map/pallas_call | solution.py:403
  43.2 125.2 %shard_map.323 = (bf16[6,1,198,768]{3,2,1,0:T(8,128)(2,1)}, bf16[1248,768]{1,0:T(8,128)(2,1)}, bf16[18,4,192,128]{3,2,1,0:T(8,128)(2,1)}, bf16[256,2304]{1,0:T(8...) custom-call(f32[1248,768]{1,0:T(8,128)} %get-tuple-element.50.mid, bf16[6,1,198,768]{3,2,1,0:T(8,128)(2,1)} %cot.1, ...), custom_call_target="tpu_custom_call" | custom-call | tf_op jit(solution)/shard_map/pallas_call | solution.py:954
  168.4 10.3 %shard_map.324 = (bf16[6,1,198,768]{3,2,1,0:T(8,128)(2,1)}, bf16[6,1,197,768]{3,2,1,0:T(8,128)(2,1)}, f32[192,768]{1,0:T(8,128)}, f32[192,2304]{1,0:T(8,128)}, f...) custom-call(bf16[18,4,192,128]{3,2,1,0:T(8,128)(2,1)} %get-tuple-ele, ...), custom_call_target="tpu_custom_call" | custom-call | tf_op jit(solution)/shard_map/pallas_call | solution.py:1059
